TPU v7x, 512 devices: a whole 4x8x8 slice. The times are simulated.
512 devices in a mesh: slab: 16 (over x_hi, y), sub: 32 (over x_lo, z, core).
Axes of the slice: x: 4 (x_hi: 2, x_lo: 2; x = x_hi * 2 + x_lo), y: 8, z: 8, core: 2. Of those that a mesh axis runs over, the one named last changes fastest.
Arguments:
- offsets: float32 [3, 4, 32, 256, 128], P(None, None, 'slab', 'sub'), may hold values from -0.5 to 0.5
- velocities: float32 [3, 4, 32, 256, 128], P(None, None, 'slab', 'sub'), may hold values from -6 to 6
- chain_label: int32 [4, 32, 256, 128], P(None, 'slab', 'sub'), may hold values from -1 to 31999, as said below
- partners: int32 [2, 4, 32, 256, 128], P(None, None, 'slab', 'sub'), may hold values from 16 to 91, as said below
- anchored: int32 [4, 32, 256, 128], P(None, 'slab', 'sub'), may hold values 0 or 1
Outputs:
- positions: float32 [3, 4, 32, 256, 128], P(None, None, 'slab', 'sub')
- half_velocity: float32 [3, 4, 32, 256, 128], P(None, None, 'slab', 'sub')
- unit_force: float32 [3, 4, 32, 256, 128], P(None, None, 'slab', 'sub')
Inputs may be any that keep to these rules, and one draw needn't show every extreme that they name: `chain_label`: beads that carry equal labels within one cell's neighbourhood belong to one loop; -1 marks an empty slot. `partners`: the two codes of a bead name the previous and the next bead of its own loop, in a neighbouring cell, and that bead names it back; every loop is closed. The codes of an empty slot are its own code.
All inputs are finite; a program needn't handle non-finite values. No bound on the sum of `anchored` on one device may be relied on, other than what follows from the above.
Results may differ from a plain program's by a relative error of at most 0.0003.
Values sent between devices are 32-bit elements; how exact they have to be, the bound alone decides.
A program may use at most 64 MiB of HBM per device.

v0:
```python
import functools

import jax
import jax.numpy as jnp
from jax import lax
from jax.sharding import Mesh
from jax.sharding import PartitionSpec as P

DESCENTS = 3
SLAB_SUB = ("slab_0", "slab_1", "sub_0", "sub_1", "sub_2")
SLAB = ("slab_0", "slab_1")
SUB = ("sub_0", "sub_1", "sub_2")


cell_width = 1.25
cutoff_sq = 2.0 ** (1.0 / 3.0)
soft_floor = 0.64
bond_stiff = 100.0
bond_inv_sq = 1.0 / 9.0
fene_floor = 0.2
time_step = 0.01
half_step = 0.005
half_step_sq = 5e-05
step_length = 0.1
tiny_eps = 1e-06


def extended(block, sides, width):
    for axis, dim in sides:
        count = lax.axis_size(axis)
        forward = [(i, i + 1) for i in range(count - 1)]
        forward.append((count - 1, 0))
        backward = [(target, source) for source, target in forward]
        low = lax.ppermute(
            lax.slice_in_dim(block, block.shape[dim] - width, None, axis=dim), axis, forward
        )
        high = lax.ppermute(lax.slice_in_dim(block, 0, width, axis=dim), axis, backward)
        block = jnp.concatenate([low, block, high], axis=dim)
    return block


def one_axis_at_a_time(value, axes):
    return functools.reduce(lax.pmax, axes, value)


def pair_force(own_pos, own_label, partner_codes, fetch_pos, fetch_label, keep_chain):
    slot_count = own_pos.shape[1]
    slot_ids = jnp.arange(slot_count, dtype=jnp.int32)
    own_live = own_label >= 0
    summed = jnp.zeros(own_pos.shape, jnp.float32)
    for offset_x in (-1, 0, 1):
        for offset_y in (-1, 0, 1):
            for offset_z in (-1, 0, 1):
                code_base = ((offset_x + 1) * 9 + (offset_y + 1) * 3 + (offset_z + 1)) * slot_count
                other_pos = fetch_pos(offset_x, offset_y, offset_z)
                other_label = fetch_label(offset_x, offset_y, offset_z)
                cell_shift = jnp.array([offset_x, offset_y, offset_z], jnp.float32) * cell_width
                separation = (
                    own_pos[:, :, None]
                    - other_pos[:, None]
                    - cell_shift[:, None, None, None, None, None]
                )
                dist_sq = jnp.sum(separation * separation, axis=0)
                pair_live = own_live[:, None] & (other_label[None] >= 0)
                if offset_x == 0 and offset_y == 0 and (offset_z == 0):
                    pair_live = pair_live & (
                        slot_ids[:, None, None, None, None] != slot_ids[None, :, None, None, None]
                    )
                bond_live = pair_live
                if not keep_chain:
                    pair_live = pair_live & (own_label[:, None] != other_label[None])
                wca_live = pair_live & (dist_sq < cutoff_sq)
                inv_two = 1.0 / jnp.maximum(dist_sq, soft_floor)
                inv_four = inv_two * inv_two
                inv_eight = inv_four * inv_four
                wca_coef = jnp.where(
                    wca_live, 24.0 * (2.0 * inv_eight * inv_four * inv_two - inv_eight), 0.0
                )
                wanted = (code_base + slot_ids)[None, None, :, None, None, None]
                matches = jnp.sum((partner_codes[:, :, None] == wanted).astype(jnp.float32), axis=0)
                fene_coef = -bond_stiff / jnp.maximum(1.0 - dist_sq * bond_inv_sq, fene_floor)
                pair_coef = wca_coef + jnp.where(bond_live, matches, 0.0) * fene_coef
                summed = summed + jnp.sum(pair_coef[None] * separation, axis=2)
    return summed


def face_coords(flat):
    return extended(flat, ((SLAB, 2), (SUB, 3)), 1)


def face_moves(flat):
    return extended(flat, ((SLAB, 2), (SUB, 3)), 1)


def local_force(wide_pos, wide_label, own_pos, own_label, partner_codes, free_mask, keep_chain):
    rows_x = own_pos.shape[2]
    rows_y = own_pos.shape[3]

    def fetch_pos(offset_x, offset_y, offset_z):
        neighbour = wide_pos[
            :, :, 1 + offset_x : 1 + offset_x + rows_x, 1 + offset_y : 1 + offset_y + rows_y
        ]
        return jnp.roll(neighbour, -offset_z, axis=4)

    def fetch_label(offset_x, offset_y, offset_z):
        neighbour = wide_label[
            :, 1 + offset_x : 1 + offset_x + rows_x, 1 + offset_y : 1 + offset_y + rows_y
        ]
        return jnp.roll(neighbour, -offset_z, axis=3)

    return (
        pair_force(own_pos, own_label, partner_codes, fetch_pos, fetch_label, keep_chain)
        * free_mask
    )


def shards(offsets, velocities, chain_label, partners, anchored):
    wide_label = extended(chain_label, ((SLAB, 1), (SUB, 2)), 1)
    free_mask = ((chain_label >= 0) & (anchored == 0)).astype(jnp.float32)
    wide_pos = face_coords(offsets)
    force_now = local_force(wide_pos, wide_label, offsets, chain_label, partners, free_mask, True)
    moving = free_mask * velocities
    motion = time_step * moving + half_step_sq * force_now
    positions = offsets + motion
    half_velocity = moving + half_step * force_now
    wide_pos = wide_pos + face_moves(motion)
    inverse = jnp.float32(1.0)
    for descent in range(DESCENTS):
        final_round = descent + 1 == DESCENTS
        force_now = local_force(
            wide_pos, wide_label, positions, chain_label, partners, free_mask, False
        )
        local_peak = jnp.max(jnp.sum(force_now * force_now, axis=0))
        if not final_round:
            wide_force = face_moves(force_now)
        peak_force = jnp.sqrt(one_axis_at_a_time(local_peak, SLAB_SUB))
        inverse = 1.0 / (peak_force + tiny_eps)
        step_scale = step_length * inverse
        positions = positions + step_scale * force_now
        if not final_round:
            wide_pos = wide_pos + step_scale * wide_force
    return (positions, half_velocity, inverse * force_now)


def solution(mesh):
    finer = Mesh(
        mesh.devices.reshape(2, 8, 2, 8, 2), ("slab_0", "slab_1", "sub_0", "sub_1", "sub_2")
    )
    in_specs = (
        P(None, None, SLAB, SUB, None),
        P(None, None, SLAB, SUB, None),
        P(None, SLAB, SUB, None),
        P(None, None, SLAB, SUB, None),
        P(None, SLAB, SUB, None),
    )
    out_specs = (
        P(None, None, SLAB, SUB, None),
        P(None, None, SLAB, SUB, None),
        P(None, None, SLAB, SUB, None),
    )
    return jax.shard_map(
        shards, mesh=finer, in_specs=in_specs, out_specs=out_specs, check_vma=False
    )
```

profile of v0, /device:TPU:1, one launch (start us, length us, event | category | flops | bytes accessed | tf_op | source)
XLA Modules:
  0.0 343.9 jit_solution(1778620172077414122)
XLA Ops:
  1.4 8.4 %collective-permute-start.1 = (s32[4,1,8,128]{3,2,1,0:T(8,128)S(1)}, s32[4,1,8,128]{3,2,1,0:T(8,128)S(1)}, u32[]{:S(2)}, u32[]{:S(2)}) collective-permute-start(s32[4,1,8,128]{3,2,1,0:T(8,128)S(1)} %get-tuple-element.644), channel_id=1, source_target_pairs={{32,0},{64,32},{96,64},{128,96},{160,128},{192,160},{224,192},{256... | collective-permute-start | bytes 49160 | tf_op jit(solution)/shard_map/ppermute | solution.py:37
  9.8 1.9 collective-permute-start
  12.5 7.0 %collective-permute-start.4 = (f32[3,4,1,8,128]{4,3,2,1,0:T(8,128)S(1)}, f32[3,4,1,8,128]{4,3,2,1,0:T(8,128)S(1)}, u32[]{:S(2)}, u32[]{:S(2)}) collective-permute-start(f32[3,4,1,8,128]{4,3,2,1,0:T(8,128)S(1)} %get-tuple-element.505), channel_id=1, source_target_pairs={{32,0},{64,32},{96,64},{128,96},{160,128},{192,160},{224,192},{256... | collective-permute-start | bytes 147464 | tf_op jit(solution)/shard_map/ppermute | solution.py:37
  19.5 1.9 collective-permute-start.3
  26.8 3.4 collective-permute-start.6
  30.2 3.9 %collective-permute-start.2 = (s32[4,4,1,128]{3,2,1,0:T(1,128)S(1)}, s32[4,4,1,128]{3,2,1,0:T(1,128)S(1)}, u32[]{:S(2)}, u32[]{:S(2)}) collective-permute-start(s32[4,4,1,128]{3,2,1,0:T(1,128)S(1)} %get-tuple-element.546), channel_id=1, source_target_pairs={{0,1},{1,2},{2,3},{3,4},{4,5},{5,6},{6,7},{7,8},{8,9},{9,10},{10,1... | collective-permute-start | bytes 24584 | tf_op jit(solution)/shard_map/ppermute | solution.py:34
  35.5 4.9 %collective-permute-done.2 = s32[4,4,1,128]{3,2,1,0:T(1,128)S(1)} collective-permute-done((s32[4,4,1,128]{3,2,1,0:T(1,128)S(1)}, s32[4,4,1,128]{3,2,1,0:T(1,128)S(1)}, u32[]{:S(2)}, u32[]{:S(2)}) %collective-permute-start.2) | collective-permute-done | bytes 8224 | tf_op jit(solution)/shard_map/ppermute | solution.py:34
  47.0 1.9 collective-permute-start.5
  49.2 6.7 %collective-permute-start.7 = (f32[3,4,4,1,128]{4,3,2,1,0:T(1,128)S(1)}, f32[3,4,4,1,128]{4,3,2,1,0:T(1,128)S(1)}, u32[]{:S(2)}, u32[]{:S(2)}) collective-permute-start(f32[3,4,4,1,128]{4,3,2,1,0:T(1,128)S(1)} %get-tuple-element.480), channel_id=1, source_target_pairs={{1,0},{2,1},{3,2},{4,3},{5,4},{6,5},{7,6},{8,7},{9,8},{10,9},{11,1... | collective-permute-start | bytes 73736 | tf_op jit(solution)/shard_map/ppermute | solution.py:37
  61.1 1.3 multiply_add_fusion.94
  62.7 1.4 multiply_add_fusion.99
  65.4 1.4 multiply_add_fusion.102
  69.5 1.4 multiply_add_fusion.89
  73.1 1.9 collective-permute-start.8
  75.1 7.6 %collective-permute-start.9 = (f32[3,4,1,8,128]{4,3,2,1,0:T(8,128)S(1)}, f32[3,4,1,8,128]{4,3,2,1,0:T(8,128)S(1)}, u32[]{:S(2)}, u32[]{:S(2)}) collective-permute-start(f32[3,4,1,8,128]{4,3,2,1,0:T(8,128)S(1)} %get-tuple-element.497), channel_id=1, source_target_pairs={{32,0},{64,32},{96,64},{128,96},{160,128},{192,160},{224,192},{256... | collective-permute-start | bytes 147464 | tf_op jit(solution)/shard_map/ppermute | solution.py:37
  83.8 1.9 collective-permute-start.10
  85.8 7.6 %collective-permute-start.11 = (f32[3,4,4,1,128]{4,3,2,1,0:T(1,128)S(1)}, f32[3,4,4,1,128]{4,3,2,1,0:T(1,128)S(1)}, u32[]{:S(2)}, u32[]{:S(2)}) collective-permute-start(f32[3,4,4,1,128]{4,3,2,1,0:T(1,128)S(1)} %get-tuple-element.475), channel_id=1, source_target_pairs={{1,0},{2,1},{3,2},{4,3},{5,4},{6,5},{7,6},{8,7},{9,8},{10,9},{11,1... | collective-permute-start | bytes 73736 | tf_op jit(solution)/shard_map/ppermute | solution.py:37
  109.8 1.9 collective-permute-start.12
  111.7 7.6 %collective-permute-start.13 = (f32[3,4,1,8,128]{4,3,2,1,0:T(8,128)S(1)}, f32[3,4,1,8,128]{4,3,2,1,0:T(8,128)S(1)}, u32[]{:S(2)}, u32[]{:S(2)}) collective-permute-start(f32[3,4,1,8,128]{4,3,2,1,0:T(8,128)S(1)} %get-tuple-element.495), channel_id=1, source_target_pairs={{32,0},{64,32},{96,64},{128,96},{160,128},{192,160},{224,192},{256... | collective-permute-start | bytes 147464 | tf_op jit(solution)/shard_map/ppermute | solution.py:37
  119.9 5.9 %pmax.105 = f32[]{:T(128)} all-reduce(f32[]{:T(128)} %reduce_max.27), channel_id=1, replica_groups=mesh['slab_0'=2,'slab_1'=8,'sub_0'=2,'sub_1'=8,'sub_2'=2] {'slab_0'}, use_global_device_ids=true, to_apply=%region_137.138 | all-reduce | flops 1 | bytes 8 | tf_op jit(solution)/shard_map/pmax | solution.py:43
  125.8 11.7 %pmax.106 = f32[]{:T(128)} all-reduce(f32[]{:T(128)} %pmax.105), channel_id=1, replica_groups=mesh['slab_0'=2,'slab_1'=8,'sub_0'=2,'sub_1'=8,'sub_2'=2] {'slab_1'}, use_global_device_ids=true, to_apply=%region_138.139 | all-reduce | flops 1 | bytes 8 | tf_op jit(solution)/shard_map/pmax | solution.py:43
  137.5 4.4 %pmax.107 = f32[]{:T(128)} all-reduce(f32[]{:T(128)} %pmax.106), channel_id=1, replica_groups=mesh['slab_0'=2,'slab_1'=8,'sub_0'=2,'sub_1'=8,'sub_2'=2] {'sub_0'}, use_global_device_ids=true, to_apply=%region_139.140 | all-reduce | flops 1 | bytes 8 | tf_op jit(solution)/shard_map/pmax | solution.py:43
  141.9 19.1 %pmax.108 = f32[]{:T(128)} all-reduce(f32[]{:T(128)} %pmax.107), channel_id=1, replica_groups=mesh['slab_0'=2,'slab_1'=8,'sub_0'=2,'sub_1'=8,'sub_2'=2] {'sub_1'}, use_global_device_ids=true, to_apply=%region_140.141 | all-reduce | flops 1 | bytes 8 | tf_op jit(solution)/shard_map/pmax | solution.py:43
  161.0 9.3 %pmax.109 = f32[]{:T(128)} all-reduce(f32[]{:T(128)} %pmax.108), channel_id=1, replica_groups=mesh['slab_0'=2,'slab_1'=8,'sub_0'=2,'sub_1'=8,'sub_2'=2] {'sub_2'}, use_global_device_ids=true, to_apply=%region_141.142 | all-reduce | flops 1 | bytes 8 | tf_op jit(solution)/shard_map/pmax | solution.py:43
  171.7 3.9 %collective-permute-start.14 = (f32[3,4,4,1,128]{4,3,2,1,0:T(1,128)S(1)}, f32[3,4,4,1,128]{4,3,2,1,0:T(1,128)S(1)}, u32[]{:S(2)}, u32[]{:S(2)}) collective-permute-start(f32[3,4,4,1,128]{4,3,2,1,0:T(1,128)S(1)} %get-tuple-element.472), channel_id=1, source_target_pairs={{0,1},{1,2},{2,3},{3,4},{4,5},{5,6},{6,7},{7,8},{8,9},{9,10},{10,1... | collective-permute-start | bytes 73736 | tf_op jit(solution)/shard_map/ppermute | solution.py:34
  175.6 2.2 collective-permute-start.15
  177.9 3.0 collective-permute-done.15
  193.2 1.3 multiply_add_fusion.41
  195.9 1.2 multiply_add_fusion.47
  198.6 1.2 multiply_add_fusion.36
  205.3 2.9 collective-permute-start.16
  208.2 6.0 %collective-permute-start.17 = (f32[3,4,1,8,128]{4,3,2,1,0:T(8,128)}, f32[3,4,1,8,128]{4,3,2,1,0:T(8,128)}, u32[]{:S(2)}, u32[]{:S(2)}) collective-permute-start(f32[3,4,1,8,128]{4,3,2,1,0:T(8,128)} %get-tuple-element.493), channel_id=1, source_target_pairs={{32,0},{64,32},{96,64},{128,96},{160,128},{192,160},{224,192},{256... | collective-permute-start | bytes 147464 | tf_op jit(solution)/shard_map/ppermute | solution.py:37
  214.8 5.9 %pmax.110 = f32[]{:T(128)} all-reduce(f32[]{:T(128)} %reduce_max.28), channel_id=1, replica_groups=mesh['slab_0'=2,'slab_1'=8,'sub_0'=2,'sub_1'=8,'sub_2'=2] {'slab_0'}, use_global_device_ids=true, to_apply=%region_198.199 | all-reduce | flops 1 | bytes 8 | tf_op jit(solution)/shard_map/pmax | solution.py:43
  220.7 11.3 %pmax.111 = f32[]{:T(128)} all-reduce(f32[]{:T(128)} %pmax.110), channel_id=1, replica_groups=mesh['slab_0'=2,'slab_1'=8,'sub_0'=2,'sub_1'=8,'sub_2'=2] {'slab_1'}, use_global_device_ids=true, to_apply=%region_199.200 | all-reduce | flops 1 | bytes 8 | tf_op jit(solution)/shard_map/pmax | solution.py:43
  231.9 4.7 %pmax.112 = f32[]{:T(128)} all-reduce(f32[]{:T(128)} %pmax.111), channel_id=1, replica_groups=mesh['slab_0'=2,'slab_1'=8,'sub_0'=2,'sub_1'=8,'sub_2'=2] {'sub_0'}, use_global_device_ids=true, to_apply=%region_200.201 | all-reduce | flops 1 | bytes 8 | tf_op jit(solution)/shard_map/pmax | solution.py:43
  236.6 14.5 %pmax.113 = f32[]{:T(128)} all-reduce(f32[]{:T(128)} %pmax.112), channel_id=1, replica_groups=mesh['slab_0'=2,'slab_1'=8,'sub_0'=2,'sub_1'=8,'sub_2'=2] {'sub_1'}, use_global_device_ids=true, to_apply=%region_201.202 | all-reduce | flops 1 | bytes 8 | tf_op jit(solution)/shard_map/pmax | solution.py:43
  251.1 9.5 %pmax.114 = f32[]{:T(128)} all-reduce(f32[]{:T(128)} %pmax.113), channel_id=1, replica_groups=mesh['slab_0'=2,'slab_1'=8,'sub_0'=2,'sub_1'=8,'sub_2'=2] {'sub_2'}, use_global_device_ids=true, to_apply=%region_202.203 | all-reduce | flops 1 | bytes 8 | tf_op jit(solution)/shard_map/pmax | solution.py:43
  262.2 3.9 %collective-permute-start.18 = (f32[3,4,4,1,128]{4,3,2,1,0:T(1,128)S(1)}, f32[3,4,4,1,128]{4,3,2,1,0:T(1,128)S(1)}, u32[]{:S(2)}, u32[]{:S(2)}) collective-permute-start(f32[3,4,4,1,128]{4,3,2,1,0:T(1,128)S(1)} %get-tuple-element.470), channel_id=1, source_target_pairs={{0,1},{1,2},{2,3},{3,4},{4,5},{5,6},{6,7},{7,8},{8,9},{9,10},{10,1... | collective-permute-start | bytes 73736 | tf_op jit(solution)/shard_map/ppermute | solution.py:34
  266.0 2.1 collective-permute-start.19
  269.2 2.0 collective-permute-done.19
  283.4 1.3 multiply_add_fusion.14
  286.1 1.2 multiply_add_fusion.20
  288.8 1.3 multiply_add_fusion.5
  294.8 5.9 %pmax.115 = f32[]{:T(128)} all-reduce(f32[]{:T(128)} %reduce_max.29), channel_id=1, replica_groups=mesh['slab_0'=2,'slab_1'=8,'sub_0'=2,'sub_1'=8,'sub_2'=2] {'slab_0'}, use_global_device_ids=true, to_apply=%region_259.260 | all-reduce | flops 1 | bytes 8 | tf_op jit(solution)/shard_map/pmax | solution.py:43
  300.7 13.0 %pmax.116 = f32[]{:T(128)} all-reduce(f32[]{:T(128)} %pmax.115), channel_id=1, replica_groups=mesh['slab_0'=2,'slab_1'=8,'sub_0'=2,'sub_1'=8,'sub_2'=2] {'slab_1'}, use_global_device_ids=true, to_apply=%region_260.261 | all-reduce | flops 1 | bytes 8 | tf_op jit(solution)/shard_map/pmax | solution.py:43
  313.8 4.7 %pmax.117 = f32[]{:T(128)} all-reduce(f32[]{:T(128)} %pmax.116), channel_id=1, replica_groups=mesh['slab_0'=2,'slab_1'=8,'sub_0'=2,'sub_1'=8,'sub_2'=2] {'sub_0'}, use_global_device_ids=true, to_apply=%region_261.262 | all-reduce | flops 1 | bytes 8 | tf_op jit(solution)/shard_map/pmax | solution.py:43
  318.4 13.9 %pmax.118 = f32[]{:T(128)} all-reduce(f32[]{:T(128)} %pmax.117), channel_id=1, replica_groups=mesh['slab_0'=2,'slab_1'=8,'sub_0'=2,'sub_1'=8,'sub_2'=2] {'sub_1'}, use_global_device_ids=true, to_apply=%region_262.263 | all-reduce | flops 1 | bytes 8 | tf_op jit(solution)/shard_map/pmax | solution.py:43
  332.3 9.9 %pmax.119 = f32[]{:T(128)} all-reduce(f32[]{:T(128)} %pmax.118), channel_id=1, replica_groups=mesh['slab_0'=2,'slab_1'=8,'sub_0'=2,'sub_1'=8,'sub_2'=2] {'sub_2'}, use_global_device_ids=true, to_apply=%region_263.264 | all-reduce | flops 1 | bytes 8 | tf_op jit(solution)/shard_map/pmax | solution.py:43
  (627 shorter events, 86.5 us)
Async XLA Ops:
  1.4 25.0 %collective-permute-start.1 = (s32[4,1,8,128]{3,2,1,0:T(8,128)S(1)}, s32[4,1,8,128]{3,2,1,0:T(8,128)S(1)}, u32[]{:S(2)}, u32[]{:S(2)}) collective-permute-start(s32[4,1,8,128]{3,2,1,0:T(8,128)S(1)} %get-tuple-element.644), channel_id=1, source_target_pairs={{32,0},{64,32},{96,64},{128,96},{160,128},{192,160},{224,192},{256... | collective-permute-start | bytes 49160 | tf_op jit(solution)/shard_map/ppermute | solution.py:37
  9.8 16.6 %collective-permute-start = (s32[4,1,8,128]{3,2,1,0:T(8,128)S(1)}, s32[4,1,8,128]{3,2,1,0:T(8,128)S(1)}, u32[]{:S(2)}, u32[]{:S(2)}) collective-permute-start(s32[4,1,8,128]{3,2,1,0:T(8,128)S(1)} %get-tuple-element.645), channel_id=1, source_target_pairs={{0,32},{32,64},{64,96},{96,128},{128,160},{160,192},{192,224},{224... | collective-permute-start | bytes 49160 | tf_op jit(solution)/shard_map/ppermute | solution.py:34
  12.5 34.0 %collective-permute-start.4 = (f32[3,4,1,8,128]{4,3,2,1,0:T(8,128)S(1)}, f32[3,4,1,8,128]{4,3,2,1,0:T(8,128)S(1)}, u32[]{:S(2)}, u32[]{:S(2)}) collective-permute-start(f32[3,4,1,8,128]{4,3,2,1,0:T(8,128)S(1)} %get-tuple-element.505), channel_id=1, source_target_pairs={{32,0},{64,32},{96,64},{128,96},{160,128},{192,160},{224,192},{256... | collective-permute-start | bytes 147464 | tf_op jit(solution)/shard_map/ppermute | solution.py:37
  19.5 27.0 %collective-permute-start.3 = (f32[3,4,1,8,128]{4,3,2,1,0:T(8,128)S(1)}, f32[3,4,1,8,128]{4,3,2,1,0:T(8,128)S(1)}, u32[]{:S(2)}, u32[]{:S(2)}) collective-permute-start(f32[3,4,1,8,128]{4,3,2,1,0:T(8,128)S(1)} %get-tuple-element.506), channel_id=1, source_target_pairs={{0,32},{32,64},{64,96},{96,128},{128,160},{160,192},{192,224},{224... | collective-permute-start | bytes 147464 | tf_op jit(solution)/shard_map/ppermute | solution.py:34
  23.3 86.2 %copy-start.24 = (f32[4,2,8,128]{3,2,1,0:T(8,128)}, f32[4,2,8,128]{3,2,1,0:T(8,128)S(1)}, u32[]{:S(2)}) copy-start(f32[4,2,8,128]{3,2,1,0:T(8,128)S(1)} %get-tuple-element.255) | copy-start | bytes 98308
  24.1 73.8 %copy-start.45 = (s32[4,2,8,128]{3,2,1,0:T(8,128)}, s32[4,2,8,128]{3,2,1,0:T(8,128)S(1)}, u32[]{:S(2)}) copy-start(s32[4,2,8,128]{3,2,1,0:T(8,128)S(1)} %get-tuple-element.724) | copy-start | bytes 98308
  24.1 80.3 %copy-start.42 = (s32[4,2,8,128]{3,2,1,0:T(8,128)}, s32[4,2,8,128]{3,2,1,0:T(8,128)S(1)}, u32[]{:S(2)}) copy-start(s32[4,2,8,128]{3,2,1,0:T(8,128)S(1)} %get-tuple-element.294) | copy-start | bytes 98308
  25.2 74.6 %copy-start.18 = (f32[4,4,2,8,128]{4,3,2,1,0:T(8,128)}, f32[4,4,2,8,128]{4,3,2,1,0:T(8,128)S(1)}, u32[]{:S(2)}) copy-start(f32[4,4,2,8,128]{4,3,2,1,0:T(8,128)S(1)} %get-tuple-element.244) | copy-start | bytes 393220
  25.2 80.9 %copy-start.2 = (f32[4,4,2,8,128]{4,3,2,1,0:T(8,128)}, f32[4,4,2,8,128]{4,3,2,1,0:T(8,128)S(1)}, u32[]{:S(2)}) copy-start(f32[4,4,2,8,128]{4,3,2,1,0:T(8,128)S(1)} %get-tuple-element.243) | copy-start | bytes 393220
  25.7 69.1 %copy-start.15 = (f32[4,4,2,8,128]{4,3,2,1,0:T(8,128)}, f32[4,4,2,8,128]{4,3,2,1,0:T(8,128)S(1)}, u32[]{:S(2)}) copy-start(f32[4,4,2,8,128]{4,3,2,1,0:T(8,128)S(1)} %get-tuple-element.230) | copy-start | bytes 393220
  25.7 72.2 %copy-start.4 = (f32[4,4,2,8,128]{4,3,2,1,0:T(8,128)}, f32[4,4,2,8,128]{4,3,2,1,0:T(8,128)S(1)}, u32[]{:S(2)}) copy-start(f32[4,4,2,8,128]{4,3,2,1,0:T(8,128)S(1)} %get-tuple-element.218) | copy-start | bytes 393220
  25.7 72.2 %copy-start.9 = (f32[4,4,2,8,128]{4,3,2,1,0:T(8,128)}, f32[4,4,2,8,128]{4,3,2,1,0:T(8,128)S(1)}, u32[]{:S(2)}) copy-start(f32[4,4,2,8,128]{4,3,2,1,0:T(8,128)S(1)} %get-tuple-element.227) | copy-start | bytes 393220
  25.7 72.2 %copy-start.12 = (f32[4,4,2,8,128]{4,3,2,1,0:T(8,128)}, f32[4,4,2,8,128]{4,3,2,1,0:T(8,128)S(1)}, u32[]{:S(2)}) copy-start(f32[4,4,2,8,128]{4,3,2,1,0:T(8,128)S(1)} %get-tuple-element.228) | copy-start | bytes 393220
  25.7 75.0 %copy-start.6 = (f32[4,4,2,8,128]{4,3,2,1,0:T(8,128)}, f32[4,4,2,8,128]{4,3,2,1,0:T(8,128)S(1)}, u32[]{:S(2)}) copy-start(f32[4,4,2,8,128]{4,3,2,1,0:T(8,128)S(1)} %get-tuple-element.226) | copy-start | bytes 393220
  26.6 75.4 %copy-start.107 = (pred[4,2,8,128]{3,2,1,0:T(8,128)(4,1)}, pred[4,2,8,128]{3,2,1,0:T(8,128)(4,1)S(1)}, u32[]{:S(2)}) copy-start(pred[4,2,8,128]{3,2,1,0:T(8,128)(4,1)S(1)} %broadcast_compare_fusion.21) | copy-start | bytes 24580
  26.8 16.0 %collective-permute-start.6 = (s32[4,4,1,128]{3,2,1,0:T(1,128)S(1)}, s32[4,4,1,128]{3,2,1,0:T(1,128)S(1)}, u32[]{:S(2)}, u32[]{:S(2)}) collective-permute-start(s32[4,4,1,128]{3,2,1,0:T(1,128)S(1)} %get-tuple-element.545), channel_id=1, source_target_pairs={{1,0},{2,1},{3,2},{4,3},{5,4},{6,5},{7,6},{8,7},{9,8},{10,9},{11,1... | collective-permute-start | bytes 24584 | tf_op jit(solution)/shard_map/ppermute | solution.py:37
  30.2 10.2 %collective-permute-start.2 = (s32[4,4,1,128]{3,2,1,0:T(1,128)S(1)}, s32[4,4,1,128]{3,2,1,0:T(1,128)S(1)}, u32[]{:S(2)}, u32[]{:S(2)}) collective-permute-start(s32[4,4,1,128]{3,2,1,0:T(1,128)S(1)} %get-tuple-element.546), channel_id=1, source_target_pairs={{0,1},{1,2},{2,3},{3,4},{4,5},{5,6},{6,7},{7,8},{8,9},{9,10},{10,1... | collective-permute-start | bytes 24584 | tf_op jit(solution)/shard_map/ppermute | solution.py:34
  34.8 71.3 %copy-start.48 = (s32[4,2,8,128]{3,2,1,0:T(8,128)}, s32[4,2,8,128]{3,2,1,0:T(8,128)S(1)}, u32[]{:S(2)}) copy-start(s32[4,2,8,128]{3,2,1,0:T(8,128)S(1)} %get-tuple-element.282) | copy-start | bytes 98308
  34.8 73.0 %copy-start.51 = (s32[4,2,8,128]{3,2,1,0:T(8,128)}, s32[4,2,8,128]{3,2,1,0:T(8,128)S(1)}, u32[]{:S(2)}) copy-start(s32[4,2,8,128]{3,2,1,0:T(8,128)S(1)} %get-tuple-element.730) | copy-start | bytes 98308
  35.5 65.3 %copy-start.66 = (s32[4,2,8,128]{3,2,1,0:T(8,128)}, s32[4,2,8,128]{3,2,1,0:T(8,128)S(1)}, u32[]{:S(2)}) copy-start(s32[4,2,8,128]{3,2,1,0:T(8,128)S(1)} %get-tuple-element.258) | copy-start | bytes 98308
  35.5 66.5 %copy-start.60 = (s32[4,2,8,128]{3,2,1,0:T(8,128)}, s32[4,2,8,128]{3,2,1,0:T(8,128)S(1)}, u32[]{:S(2)}) copy-start(s32[4,2,8,128]{3,2,1,0:T(8,128)S(1)} %get-tuple-element.726) | copy-start | bytes 98308
  41.4 59.4 %copy-start.90 = (s32[4,2,8,128]{3,2,1,0:T(8,128)}, s32[4,2,8,128]{3,2,1,0:T(8,128)S(1)}, u32[]{:S(2)}) copy-start(s32[4,2,8,128]{3,2,1,0:T(8,128)S(1)} %get-tuple-element.722) | copy-start | bytes 98308
  42.1 65.7 %copy-start.54 = (s32[4,2,8,128]{3,2,1,0:T(8,128)}, s32[4,2,8,128]{3,2,1,0:T(8,128)S(1)}, u32[]{:S(2)}) copy-start(s32[4,2,8,128]{3,2,1,0:T(8,128)S(1)} %get-tuple-element.276) | copy-start | bytes 98308
  42.1 65.8 %copy-start.57 = (s32[4,2,8,128]{3,2,1,0:T(8,128)}, s32[4,2,8,128]{3,2,1,0:T(8,128)S(1)}, u32[]{:S(2)}) copy-start(s32[4,2,8,128]{3,2,1,0:T(8,128)S(1)} %get-tuple-element.720) | copy-start | bytes 98308
  44.4 59.9 %copy-start.63 = (s32[4,2,8,128]{3,2,1,0:T(8,128)}, s32[4,2,8,128]{3,2,1,0:T(8,128)S(1)}, u32[]{:S(2)}) copy-start(s32[4,2,8,128]{3,2,1,0:T(8,128)S(1)} %get-tuple-element.300) | copy-start | bytes 98308
  44.4 59.9 %copy-start.84 = (s32[4,2,8,128]{3,2,1,0:T(8,128)}, s32[4,2,8,128]{3,2,1,0:T(8,128)S(1)}, u32[]{:S(2)}) copy-start(s32[4,2,8,128]{3,2,1,0:T(8,128)S(1)} %get-tuple-element.708) | copy-start | bytes 98308
  45.1 61.0 %copy-start.72 = (s32[4,2,8,128]{3,2,1,0:T(8,128)}, s32[4,2,8,128]{3,2,1,0:T(8,128)S(1)}, u32[]{:S(2)}) copy-start(s32[4,2,8,128]{3,2,1,0:T(8,128)S(1)} %get-tuple-element.706) | copy-start | bytes 98308
  45.8 58.6 %copy-start.33 = (s32[4,2,8,128]{3,2,1,0:T(8,128)}, s32[4,2,8,128]{3,2,1,0:T(8,128)S(1)}, u32[]{:S(2)}) copy-start(s32[4,2,8,128]{3,2,1,0:T(8,128)S(1)} %get-tuple-element.520) | copy-start | bytes 98308
  45.8 58.6 %copy-start.116 = (pred[4,2,8,128]{3,2,1,0:T(8,128)(4,1)}, pred[4,2,8,128]{3,2,1,0:T(8,128)(4,1)S(1)}, u32[]{:S(2)}) copy-start(pred[4,2,8,128]{3,2,1,0:T(8,128)(4,1)S(1)} %get-tuple-element.519) | copy-start | bytes 24580
  45.8 60.3 %copy-start.99 = (s32[4,2,8,128]{3,2,1,0:T(8,128)}, s32[4,2,8,128]{3,2,1,0:T(8,128)S(1)}, u32[]{:S(2)}) copy-start(s32[4,2,8,128]{3,2,1,0:T(8,128)S(1)} %get-tuple-element.522) | copy-start | bytes 98308
  45.8 62.0 %copy-start.27 = (s32[4,2,8,128]{3,2,1,0:T(8,128)}, s32[4,2,8,128]{3,2,1,0:T(8,128)S(1)}, u32[]{:S(2)}) copy-start(s32[4,2,8,128]{3,2,1,0:T(8,128)S(1)} %get-tuple-element.540) | copy-start | bytes 98308
  45.8 62.0 %copy-start.110 = (pred[4,2,8,128]{3,2,1,0:T(8,128)(4,1)}, pred[4,2,8,128]{3,2,1,0:T(8,128)(4,1)S(1)}, u32[]{:S(2)}) copy-start(pred[4,2,8,128]{3,2,1,0:T(8,128)(4,1)S(1)} %get-tuple-element.539) | copy-start | bytes 24580
  47.0 8.9 %collective-permute-start.5 = (f32[3,4,4,1,128]{4,3,2,1,0:T(1,128)S(1)}, f32[3,4,4,1,128]{4,3,2,1,0:T(1,128)S(1)}, u32[]{:S(2)}, u32[]{:S(2)}) collective-permute-start(f32[3,4,4,1,128]{4,3,2,1,0:T(1,128)S(1)} %get-tuple-element.481), channel_id=1, source_target_pairs={{0,1},{1,2},{2,3},{3,4},{4,5},{5,6},{6,7},{7,8},{8,9},{9,10},{10,1... | collective-permute-start | bytes 73736 | tf_op jit(solution)/shard_map/ppermute | solution.py:34
  49.2 7.4 %collective-permute-start.7 = (f32[3,4,4,1,128]{4,3,2,1,0:T(1,128)S(1)}, f32[3,4,4,1,128]{4,3,2,1,0:T(1,128)S(1)}, u32[]{:S(2)}, u32[]{:S(2)}) collective-permute-start(f32[3,4,4,1,128]{4,3,2,1,0:T(1,128)S(1)} %get-tuple-element.480), channel_id=1, source_target_pairs={{1,0},{2,1},{3,2},{4,3},{5,4},{6,5},{7,6},{8,7},{9,8},{10,9},{11,1... | collective-permute-start | bytes 73736 | tf_op jit(solution)/shard_map/ppermute | solution.py:37
  73.1 9.5 %collective-permute-start.8 = (f32[3,4,1,8,128]{4,3,2,1,0:T(8,128)S(1)}, f32[3,4,1,8,128]{4,3,2,1,0:T(8,128)S(1)}, u32[]{:S(2)}, u32[]{:S(2)}) collective-permute-start(f32[3,4,1,8,128]{4,3,2,1,0:T(8,128)S(1)} %get-tuple-element.496), channel_id=1, source_target_pairs={{0,32},{32,64},{64,96},{96,128},{128,160},{160,192},{192,224},{224... | collective-permute-start | bytes 147464 | tf_op jit(solution)/shard_map/ppermute | solution.py:34
  75.1 8.7 %collective-permute-start.9 = (f32[3,4,1,8,128]{4,3,2,1,0:T(8,128)S(1)}, f32[3,4,1,8,128]{4,3,2,1,0:T(8,128)S(1)}, u32[]{:S(2)}, u32[]{:S(2)}) collective-permute-start(f32[3,4,1,8,128]{4,3,2,1,0:T(8,128)S(1)} %get-tuple-element.497), channel_id=1, source_target_pairs={{32,0},{64,32},{96,64},{128,96},{160,128},{192,160},{224,192},{256... | collective-permute-start | bytes 147464 | tf_op jit(solution)/shard_map/ppermute | solution.py:37
  83.8 9.6 %collective-permute-start.10 = (f32[3,4,4,1,128]{4,3,2,1,0:T(1,128)S(1)}, f32[3,4,4,1,128]{4,3,2,1,0:T(1,128)S(1)}, u32[]{:S(2)}, u32[]{:S(2)}) collective-permute-start(f32[3,4,4,1,128]{4,3,2,1,0:T(1,128)S(1)} %get-tuple-element.474), channel_id=1, source_target_pairs={{0,1},{1,2},{2,3},{3,4},{4,5},{5,6},{6,7},{7,8},{8,9},{9,10},{10,1... | collective-permute-start | bytes 73736 | tf_op jit(solution)/shard_map/ppermute | solution.py:34
  85.8 7.9 %collective-permute-start.11 = (f32[3,4,4,1,128]{4,3,2,1,0:T(1,128)S(1)}, f32[3,4,4,1,128]{4,3,2,1,0:T(1,128)S(1)}, u32[]{:S(2)}, u32[]{:S(2)}) collective-permute-start(f32[3,4,4,1,128]{4,3,2,1,0:T(1,128)S(1)} %get-tuple-element.475), channel_id=1, source_target_pairs={{1,0},{2,1},{3,2},{4,3},{5,4},{6,5},{7,6},{8,7},{9,8},{10,9},{11,1... | collective-permute-start | bytes 73736 | tf_op jit(solution)/shard_map/ppermute | solution.py:37
  109.8 68.1 %copy-start.21 = (f32[3,4,2,8,128]{4,3,2,1,0:T(8,128)}, f32[3,4,2,8,128]{4,3,2,1,0:T(8,128)S(1)}, u32[]{:S(2)}) copy-start(f32[3,4,2,8,128]{4,3,2,1,0:T(8,128)S(1)} %get-tuple-element.252) | copy-start | bytes 294916
  109.8 61.3 %collective-permute-start.12 = (f32[3,4,1,8,128]{4,3,2,1,0:T(8,128)S(1)}, f32[3,4,1,8,128]{4,3,2,1,0:T(8,128)S(1)}, u32[]{:S(2)}, u32[]{:S(2)}) collective-permute-start(f32[3,4,1,8,128]{4,3,2,1,0:T(8,128)S(1)} %get-tuple-element.494), channel_id=1, source_target_pairs={{0,32},{32,64},{64,96},{96,128},{128,160},{160,192},{192,224},{224... | collective-permute-start | bytes 147464 | tf_op jit(solution)/shard_map/ppermute | solution.py:34
  111.7 59.4 %collective-permute-start.13 = (f32[3,4,1,8,128]{4,3,2,1,0:T(8,128)S(1)}, f32[3,4,1,8,128]{4,3,2,1,0:T(8,128)S(1)}, u32[]{:S(2)}, u32[]{:S(2)}) collective-permute-start(f32[3,4,1,8,128]{4,3,2,1,0:T(8,128)S(1)} %get-tuple-element.495), channel_id=1, source_target_pairs={{32,0},{64,32},{96,64},{128,96},{160,128},{192,160},{224,192},{256... | collective-permute-start | bytes 147464 | tf_op jit(solution)/shard_map/ppermute | solution.py:37
  171.7 6.2 %collective-permute-start.14 = (f32[3,4,4,1,128]{4,3,2,1,0:T(1,128)S(1)}, f32[3,4,4,1,128]{4,3,2,1,0:T(1,128)S(1)}, u32[]{:S(2)}, u32[]{:S(2)}) collective-permute-start(f32[3,4,4,1,128]{4,3,2,1,0:T(1,128)S(1)} %get-tuple-element.472), channel_id=1, source_target_pairs={{0,1},{1,2},{2,3},{3,4},{4,5},{5,6},{6,7},{7,8},{8,9},{9,10},{10,1... | collective-permute-start | bytes 73736 | tf_op jit(solution)/shard_map/ppermute | solution.py:34
  175.6 5.3 %collective-permute-start.15 = (f32[3,4,4,1,128]{4,3,2,1,0:T(1,128)S(1)}, f32[3,4,4,1,128]{4,3,2,1,0:T(1,128)S(1)}, u32[]{:S(2)}, u32[]{:S(2)}) collective-permute-start(f32[3,4,4,1,128]{4,3,2,1,0:T(1,128)S(1)} %get-tuple-element.473), channel_id=1, source_target_pairs={{1,0},{2,1},{3,2},{4,3},{5,4},{6,5},{7,6},{8,7},{9,8},{10,9},{11,1... | collective-permute-start | bytes 73736 | tf_op jit(solution)/shard_map/ppermute | solution.py:37
  204.6 61.4 %copy-start.22 = (f32[3,4,2,8,128]{4,3,2,1,0:T(8,128)}, f32[3,4,2,8,128]{4,3,2,1,0:T(8,128)S(1)}, u32[]{:S(2)}) copy-start(f32[3,4,2,8,128]{4,3,2,1,0:T(8,128)S(1)} %get-tuple-element.250) | copy-start | bytes 294916
  205.3 55.9 %collective-permute-start.16 = (f32[3,4,1,8,128]{4,3,2,1,0:T(8,128)}, f32[3,4,1,8,128]{4,3,2,1,0:T(8,128)}, u32[]{:S(2)}, u32[]{:S(2)}) collective-permute-start(f32[3,4,1,8,128]{4,3,2,1,0:T(8,128)} %get-tuple-element.492), channel_id=1, source_target_pairs={{0,32},{32,64},{64,96},{96,128},{128,160},{160,192},{192,224},{224... | collective-permute-start | bytes 147464 | tf_op jit(solution)/shard_map/ppermute | solution.py:34
  208.2 53.0 %collective-permute-start.17 = (f32[3,4,1,8,128]{4,3,2,1,0:T(8,128)}, f32[3,4,1,8,128]{4,3,2,1,0:T(8,128)}, u32[]{:S(2)}, u32[]{:S(2)}) collective-permute-start(f32[3,4,1,8,128]{4,3,2,1,0:T(8,128)} %get-tuple-element.493), channel_id=1, source_target_pairs={{32,0},{64,32},{96,64},{128,96},{160,128},{192,160},{224,192},{256... | collective-permute-start | bytes 147464 | tf_op jit(solution)/shard_map/ppermute | solution.py:37
  262.2 7.0 %collective-permute-start.18 = (f32[3,4,4,1,128]{4,3,2,1,0:T(1,128)S(1)}, f32[3,4,4,1,128]{4,3,2,1,0:T(1,128)S(1)}, u32[]{:S(2)}, u32[]{:S(2)}) collective-permute-start(f32[3,4,4,1,128]{4,3,2,1,0:T(1,128)S(1)} %get-tuple-element.470), channel_id=1, source_target_pairs={{0,1},{1,2},{2,3},{3,4},{4,5},{5,6},{6,7},{7,8},{8,9},{9,10},{10,1... | collective-permute-start | bytes 73736 | tf_op jit(solution)/shard_map/ppermute | solution.py:34
  266.0 5.1 %collective-permute-start.19 = (f32[3,4,4,1,128]{4,3,2,1,0:T(1,128)S(1)}, f32[3,4,4,1,128]{4,3,2,1,0:T(1,128)S(1)}, u32[]{:S(2)}, u32[]{:S(2)}) collective-permute-start(f32[3,4,4,1,128]{4,3,2,1,0:T(1,128)S(1)} %get-tuple-element.471), channel_id=1, source_target_pairs={{1,0},{2,1},{3,2},{4,3},{5,4},{6,5},{7,6},{8,7},{9,8},{10,9},{11,1... | collective-permute-start | bytes 73736 | tf_op jit(solution)/shard_map/ppermute | solution.py:37
  (172 other events, 813.0 us)
where the time goes:
time: 350 us; the launch traced here: 344 us
  blocking collectives  144 us (41%)
  starting transfers between devices  84.6 us (24%)
  other arithmetic  75.6 us (22%)
  local copies, waits for them, and re-layouts  22.4 us (6%)
  waiting for transfers between devices  11.4 us (3%)
  between operations  6.3 us (2%)
    pmax x15, blocking collectives, one_axis_at_a_time(): return functools.reduce(lax.pmax, axes, value)  144 us
    ppermute x10, starting transfers between devices, extended(): lax.ppermute(lax.slice_in_dim(block, 0, width, axis=dim), axis, backward)  58.6 us
    add x31, other arithmetic, pair_force(): pair_coef = wca_coef + jnp.where(bond_live, matches, 0.0) * fene_coef  35.3 us
    ppermute x10, starting transfers between devices, extended(): lax.ppermute(lax.slice_in_dim(block, block.shape[dim] - width, None, axis...  26 us
    unnamed x403, local copies, waits for them, and re-layouts  17 us
    reduce_sum x24, other arithmetic, pair_force(): summed = summed + jnp.sum(pair_coef[None] * separation, axis=2)  11.9 us
    ge x13, other arithmetic, pair_force(): pair_live = own_live[:, None] & (other_label[None] >= 0)  7.58 us
  transfers between devices with their start and end apart: 20, of which 5 were waited for; matrix products, arithmetic and copies ran while one was open for 4% of the time, Pallas kernels for 0%

commit v1 on v0

v1 whole, which is shorter than its diff:
```python
import jax
import jax.numpy as jnp
from jax import lax
from jax.experimental import pallas as pl
from jax.experimental.pallas import tpu as pltpu
from jax.sharding import PartitionSpec as P

MESH = pl.DeviceIdType.MESH
SLOTS = 4
PARTS = 12
NSLAB, NSUB = 16, 32
HALF = 16
N1, N2 = 15, 31

cell_width = 1.25
soft_floor = 0.64
bond_stiff = 100.0
time_step = 0.01
half_step = 0.005
half_step_sq = 5e-05
step_length = 0.1
tiny_eps = 1e-06
away = 1.0e4
no_pair = 1.0e3
FORCE_UNIT = 48.0
BOND = -bond_stiff * 9.0 / FORCE_UNIT


def kernel(
    off_in,
    vel_in,
    lab_in,
    par_in,
    anc_in,
    pos_out,
    half_out,
    unit_out,
    off,
    vel,
    lab,
    par,
    anc,
    box,
    labels,
    rows_out,
    rows_in,
    bond,
    floors,
    acc,
    free,
    mine,
    slots,
    load_sem,
    face_send,
    face_recv,
    max_send,
    max_recv,
):
    slab = lax.axis_index("slab")
    sub = lax.axis_index("sub")
    around = (
        (1, 0),
        (-1, 0),
        (0, 1),
        (0, -1),
        (1, 1),
        (1, -1),
        (-1, 1),
        (-1, -1),
    )
    near = [((slab + u + NSLAB) % NSLAB, (sub + v + NSUB) % NSUB) for u, v in around]
    low, part = sub % HALF, sub // HALF
    line = [(slab, part * HALF + (low + d) % HALF) for d in range(1, N1 + 1)]
    place = part * NSLAB + slab
    plane_peers = []
    for d in range(1, N2 + 1):
        there = (place + d) % (NSLAB * 2)
        plane_peers.append((there % NSLAB, (there // NSLAB) * HALF + low))

    barrier = pltpu.get_barrier_semaphore()
    everyone = near + line + plane_peers
    for device in everyone:
        pl.semaphore_signal(barrier, inc=1, device_id=device, device_id_type=MESH)

    loads = [
        pltpu.make_async_copy(source, target, load_sem.at[k])
        for k, (source, target) in enumerate(
            ((off_in, off), (lab_in, lab), (par_in, par), (vel_in, vel), (anc_in, anc))
        )
    ]
    for copy in loads:
        copy.start()

    blank = jnp.zeros((PARTS, 8, 128), jnp.float32)

    def clear(q, carry):
        for e in range(4):
            box[e, q, :, 0:8, :] = blank
            box[e, q, :, 16:24, :] = blank
        labels[q, :, 0:8, :] = blank[:SLOTS]
        labels[q, :, 16:24, :] = blank[:SLOTS]
        return carry

    lax.fori_loop(0, 4, clear, 0)
    rows_out[...] = jnp.zeros(rows_out.shape, jnp.float32)

    loads[0].wait()
    loads[1].wait()
    for p in range(2):
        for j in range(SLOTS):
            label = lab[j, p]
            labels[p + 1, j, 8:16, :] = label.astype(jnp.float32)
            box[0, p + 1, j, 8:16, :] = off[0, j, p] + jnp.where(label < 0, away, 0.0)
            for c in (1, 2):
                box[0, p + 1, c * SLOTS + j, 8:16, :] = off[c, j, p]

    def pack(e):
        for side, row in ((0, 8), (1, 15)):
            for p in range(2):
                for k in range(PARTS):
                    rows_out[e, side, p, k : k + 1, :] = box[e, p + 1, k, row : row + 1, :]

    pack(0)
    for side, row in ((0, 8), (1, 15)):
        for p in range(2):
            for j in range(SLOTS):
                rows_out[0, side, p, PARTS + j : PARTS + j + 1, :] = labels[
                    p + 1, j, row : row + 1, :
                ]

    loads[2].wait()

    def bonds(t, carry):
        p = t // 9
        g = t % 9
        for ez in range(3):
            for j in range(SLOTS):
                wanted = (g * 3 + ez) * SLOTS + j
                for i in range(SLOTS):
                    bond[p, g, ez, j, i] = jnp.where(par[0, i, p] == wanted, BOND, 0.0) + jnp.where(
                        par[1, i, p] == wanted, BOND, 0.0
                    )
        return carry

    lax.fori_loop(0, 18, bonds, 0)
    loads[3].wait()
    loads[4].wait()
    for p in range(2):
        for i in range(SLOTS):
            free[p, i] = jnp.where((lab[i, p] >= 0) & (anc[i, p] == 0), 1.0, 0.0)

    pl.semaphore_wait(barrier, len(everyone))

    def face(e, k, source, target):
        return pltpu.make_async_remote_copy(
            src_ref=source,
            dst_ref=target,
            send_sem=face_send.at[e, k],
            recv_sem=face_recv.at[e, k],
            device_id=near[k % 8],
            device_id_type=MESH,
        )

    def planes(e, p):
        return face(
            e,
            1 - p,
            box.at[e, p + 1, :, 8:16, :],
            box.at[e, 3 - 3 * p, :, 8:16, :],
        )

    def edges(e):
        return [
            face(e, 2, rows_out.at[e, 1], rows_in.at[e, 0, 1:3]),
            face(e, 3, rows_out.at[e, 0], rows_in.at[e, 1, 1:3]),
            face(e, 4, rows_out.at[e, 1, 1], rows_in.at[e, 0, 0]),
            face(e, 5, rows_out.at[e, 0, 1], rows_in.at[e, 1, 0]),
            face(e, 6, rows_out.at[e, 1, 0], rows_in.at[e, 0, 3]),
            face(e, 7, rows_out.at[e, 0, 0], rows_in.at[e, 1, 3]),
        ]

    label_faces = [
        face(0, 9 - p, labels.at[p + 1, :, 8:16, :], labels.at[3 - 3 * p, :, 8:16, :])
        for p in range(2)
    ]
    face_copies = [[planes(e, 0), planes(e, 1)] for e in range(4)]
    edge_copies = [edges(e) for e in range(4)]

    def unpack(e):
        def one(q, carry):
            for side, row in ((0, 7), (1, 16)):
                for k in range(PARTS):
                    box[e, q, k, row : row + 1, :] = rows_in[e, side, q, k : k + 1, :]
            return carry

        lax.fori_loop(0, 4, one, 0)

    def group(e, p, q, ey, fresh):
        ex = (q - p - 1).astype(jnp.float32) * cell_width
        g = 3 * (q - p) + (ey + 1)
        own = [
            [box[e, p + 1, c * SLOTS + i, 8:16, :] for i in range(SLOTS)] for c in range(3)
        ]
        total = [
            [
                jnp.zeros((8, 128), jnp.float32) if fresh else acc[p, c * SLOTS + i]
                for i in range(SLOTS)
            ]
            for c in range(3)
        ]
        own_x = [own[0][i] - ex for i in range(SLOTS)]
        own_y = [own[1][i] - ey * cell_width for i in range(SLOTS)]
        for ez in (-1, 0, 1):
            own_z = [own[2][i] - ez * cell_width for i in range(SLOTS)]
            for j in range(SLOTS):
                other = [box[e, q, c * SLOTS + j, 8 + ey : 16 + ey, :] for c in range(3)]
                if ez != 0:
                    other = [pltpu.roll(o, (-ez) % 128, 1) for o in other]
                for i in range(SLOTS):
                    sx = own_x[i] - other[0]
                    sy = own_y[i] - other[1]
                    sz = own_z[i] - other[2]
                    dist = sx * sx + sy * sy + sz * sz
                    least = soft_floor if e == 0 else floors[p, g, ez + 1, j, i]
                    q1 = pl.reciprocal(jnp.maximum(dist, least), approx=True)
                    q2 = q1 * q1
                    q3 = q2 * q1
                    q4 = q2 * q2
                    push = q4 * jnp.maximum(q3 - 0.5, 0.0)
                    pull = bond[p, g, ez + 1, j, i] * pl.reciprocal(
                        jnp.maximum(9.0 - dist, 1.8), approx=True
                    )
                    coef = push + pull
                    total[0][i] = total[0][i] + coef * sx
                    total[1][i] = total[1][i] + coef * sy
                    total[2][i] = total[2][i] + coef * sz
        for c in range(3):
            for i in range(SLOTS):
                acc[p, c * SLOTS + i] = total[c][i]

    def inner(e):
        def first(p, carry):
            group(e, p, p + 1, 0, True)
            return carry

        def second(p, carry):
            group(e, p, 2 - p, 0, False)
            return carry

        lax.fori_loop(0, 2, first, 0)
        lax.fori_loop(0, 2, second, 0)

    def sides(e):
        def one(t, carry):
            for ey in (-1, 1):
                group(e, t // 2, 1 + t % 2, ey, False)
            return carry

        lax.fori_loop(0, 4, one, 0)

    def outer(e):
        def one(p, carry):
            for ey in (-1, 0, 1):
                group(e, p, 3 * p, ey, False)
            return carry

        lax.fori_loop(0, 2, one, 0)

    def limits():
        def one(t, carry):
            p = t // 3
            for ey in (-1, 0, 1):
                g = 3 * (t % 3) + (ey + 1)
                for ez in (-1, 0, 1):
                    for j in range(SLOTS):
                        other = labels[p + t % 3, j, 8 + ey : 16 + ey, :]
                        if ez != 0:
                            other = pltpu.roll(other, (-ez) % 128, 1)
                        for i in range(SLOTS):
                            floors[p, g, ez + 1, j, i] = jnp.where(
                                labels[p + 1, i, 8:16, :] == other, no_pair, soft_floor
                            )
            return carry

        lax.fori_loop(0, 6, one, 0)

    def global_max(r, value):
        row = jnp.max(value, axis=0, keepdims=True)
        base = 0
        for phase, peers in enumerate((line, plane_peers)):
            mine[r, phase] = row
            copies = [
                pltpu.make_async_remote_copy(
                    src_ref=mine.at[r, phase],
                    dst_ref=slots.at[r, base + k],
                    send_sem=max_send.at[r, base + k],
                    recv_sem=max_recv.at[r, base + k],
                    device_id=device,
                    device_id_type=MESH,
                )
                for k, device in enumerate(peers)
            ]
            for copy in copies:
                copy.start()
            yield copies
            for copy in copies:
                copy.wait_recv()
            row = jnp.maximum(row, jnp.max(slots[r, base : base + len(peers)], axis=0))
            base += len(peers)
        yield jnp.max(row, axis=1, keepdims=True)

    for copy in face_copies[0] + edge_copies[0] + label_faces:
        copy.start()
    inner(0)
    for copy in edge_copies[0]:
        copy.wait_recv()
    unpack(0)
    sides(0)
    for copy in face_copies[0]:
        copy.wait_recv()
    outer(0)
    for p in range(2):
        for c in range(3):
            for i in range(SLOTS):
                k = c * SLOTS + i
                force = acc[p, k] * FORCE_UNIT * free[p, i]
                moving = free[p, i] * vel[c, i, p]
                half_out[c, i, p] = moving + half_step * force
                box[1, p + 1, k, 8:16, :] = box[0, p + 1, k, 8:16, :] + (
                    time_step * moving + half_step_sq * force
                )
        face_copies[1][p].start()
    pack(1)
    for copy in edge_copies[1]:
        copy.start()
    for copy in label_faces:
        copy.wait_recv()

    def label_rows(q, carry):
        for side, row in ((0, 7), (1, 16)):
            for j in range(SLOTS):
                labels[q, j, row : row + 1, :] = rows_in[
                    0, side, q, PARTS + j : PARTS + j + 1, :
                ]
        return carry

    lax.fori_loop(0, 4, label_rows, 0)
    limits()
    inner(1)
    for copy in edge_copies[1]:
        copy.wait_recv()
    unpack(1)
    sides(1)
    for copy in face_copies[1]:
        copy.wait_recv()

    started = face_copies[0] + edge_copies[0] + label_faces + edge_copies[1]
    for r in range(3):
        if r > 0:
            inner(1)
            sides(1)
        outer(1)
        final = r == 2
        peak = jnp.zeros((8, 128), jnp.float32)
        for p in range(2):
            for i in range(SLOTS):
                size = jnp.zeros((8, 128), jnp.float32)
                for c in range(3):
                    k = c * SLOTS + i
                    force = acc[p, k] * FORCE_UNIT * free[p, i]
                    size = size + force * force
                    if final:
                        unit_out[c, i, p] = force
                    else:
                        box[r + 2, p + 1, k, 8:16, :] = force
                peak = jnp.maximum(peak, size)
        steps = global_max(r, peak)
        started += next(steps)
        if not final:
            for copy in face_copies[r + 2]:
                copy.start()
            pack(r + 2)
            for copy in edge_copies[r + 2]:
                copy.start()
            started += face_copies[r + 2] + edge_copies[r + 2]
        started += next(steps)
        if not final:
            for copy in edge_copies[r + 2]:
                copy.wait_recv()
            unpack(r + 2)
            for copy in face_copies[r + 2]:
                copy.wait_recv()
        largest = next(steps)
        inverse = 1.0 / (jnp.sqrt(largest) + tiny_eps)
        scale = step_length * inverse
        if not final:
            if r == 0:
                for copy in face_copies[1]:
                    copy.wait_send()

            def move(q, carry):
                box[1, q] = box[1, q] + scale * box[r + 2, q]
                return carry

            lax.fori_loop(0, 4, move, 0)
        else:
            for p in range(2):
                for c in range(3):
                    for i in range(SLOTS):
                        force = unit_out[c, i, p]
                        place_now = box[1, p + 1, c * SLOTS + i, 8:16, :] + scale * force
                        if c == 0:
                            place_now = jnp.where(lab[i, p] < 0, off[c, i, p], place_now)
                        pos_out[c, i, p] = place_now
                        unit_out[c, i, p] = inverse * force
    for copy in started:
        copy.wait_send()


def shards(offsets, velocities, chain_label, partners, anchored):
    shape = jax.ShapeDtypeStruct(offsets.shape, jnp.float32)
    f32 = jnp.float32
    return tuple(
        pl.pallas_call(
            kernel,
            out_shape=(shape, shape, shape),
            in_specs=[pl.BlockSpec(memory_space=pl.ANY)] * 5,
            out_specs=[pl.BlockSpec(memory_space=pltpu.VMEM)] * 3,
            scratch_shapes=[
                pltpu.VMEM(offsets.shape, f32),
                pltpu.VMEM(velocities.shape, f32),
                pltpu.VMEM(chain_label.shape, jnp.int32),
                pltpu.VMEM(partners.shape, jnp.int32),
                pltpu.VMEM(anchored.shape, jnp.int32),
                pltpu.VMEM((4, 4, PARTS, 24, 128), f32),
                pltpu.VMEM((4, SLOTS, 24, 128), f32),
                pltpu.VMEM((4, 2, 2, 16, 128), f32),
                pltpu.VMEM((4, 2, 4, 16, 128), f32),
                pltpu.VMEM((2, 9, 3, SLOTS, SLOTS, 8, 128), f32),
                pltpu.VMEM((2, 9, 3, SLOTS, SLOTS, 8, 128), f32),
                pltpu.VMEM((2, PARTS, 8, 128), f32),
                pltpu.VMEM((2, SLOTS, 8, 128), f32),
                pltpu.VMEM((3, 2, 1, 128), f32),
                pltpu.VMEM((3, N1 + N2, 1, 128), f32),
                pltpu.SemaphoreType.DMA((5,)),
                pltpu.SemaphoreType.DMA((4, 10)),
                pltpu.SemaphoreType.DMA((4, 10)),
                pltpu.SemaphoreType.DMA((3, N1 + N2)),
                pltpu.SemaphoreType.DMA((3, N1 + N2)),
            ],
            compiler_params=pltpu.CompilerParams(
                collective_id=0, has_side_effects=True, vmem_limit_bytes=24 * 1024 * 1024
            ),
        )(offsets, velocities, chain_label, partners, anchored)
    )


def solution(mesh):
    whole = P(None, None, "slab", "sub", None)
    labels = P(None, "slab", "sub", None)
    return jax.shard_map(
        shards,
        mesh=mesh,
        in_specs=(whole, whole, labels, whole, labels),
        out_specs=(whole, whole, whole),
        check_vma=False,
    )
```

time: 350 us -> 79.2 us (0.23); the launches traced: 344 us -> 78.9 us
  blocking collectives: 144 us -> 0 us
  starting transfers between devices: 84.6 us -> 0 us
  other arithmetic: 75.6 us -> 0 us
  Pallas kernels: 0 us -> 72.1 us
  local copies, waits for them, and re-layouts: 22.4 us -> 6.05 us
  waiting for transfers between devices: 11.4 us -> 0 us
  between operations: 6.3 us -> 0.65 us
    pmax x15 -> x0, blocking collectives: 144 us -> none  [one_axis_at_a_time(): return functools.reduce(lax.pmax, axes, value)]
    ppermute x20 -> x0, starting transfers between devices: 84.6 us -> none  [the longest x10 58.6 us: extended(): lax.ppermute(lax.slice_in_dim(block, 0, width, axis=dim), axis, backward)]
    pallas_call x0 -> x1, Pallas kernels: none -> 72.1 us  [shards(): pl.pallas_call(kernel, out_shape=(shape, shape, shape), in_specs=[pl.Bloc...]
    add x51 -> x0, other arithmetic: 39.3 us -> none  [the longest x31 35.3 us: pair_force(): pair_coef = wca_coef + jnp.where(bond_live, matches, 0.0) * fene_coef]
    reduce_sum x37 -> x0, other arithmetic: 17.1 us -> none  [the longest x24 11.9 us: pair_force(): summed = summed + jnp.sum(pair_coef[None] * separation, axis=2)]
    ppermute x20 -> x0, waiting for transfers between devices: 11.4 us -> none  [the longest x10 6.42 us: extended(): lax.ppermute(lax.slice_in_dim(block, 0, width, axis=dim), axis, backward)]
    unnamed x403 -> x13, local copies, waits for them, and re-layouts: 17 us -> 6.05 us
    ge x13 -> x0, other arithmetic: 7.58 us -> none  [pair_force(): pair_live = own_live[:, None] & (other_label[None] >= 0)]
  transfers between devices with their start and end apart: 20 -> 0, of which waited for: 5 -> 0; matrix products, arithmetic and copies ran while one was open for 4% -> 0% of each run, Pallas kernels for 0% -> 0%
where the time goes in v1:
time: 79.2 us; the launch traced here: 78.9 us
  Pallas kernels  72.1 us (91%)
  local copies, waits for them, and re-layouts  6.05 us (8%)
    pallas_call x1, Pallas kernels, shards(): pl.pallas_call(kernel, out_shape=(shape, shape, shape), in_specs=[pl.Bloc...  72.1 us
    unnamed x13, local copies, waits for them, and re-layouts  6.05 us

profile of v1, /device:TPU:1, one launch (start us, length us, event | category | flops | bytes accessed | tf_op | source)
XLA Modules:
  0.0 78.9 jit_solution(6164386442051260944)
XLA Ops:
  0.6 0.0 copy-start
  0.6 0.9 %copy-done = f32[3,4,2,8,128]{4,3,2,1,0:T(8,128)S(1)} copy-done((f32[3,4,2,8,128]{4,3,2,1,0:T(8,128)S(1)}, f32[3,4,2,8,128]{4,3,2,1,0:T(8,128)}, u32[]{:S(2)}) %copy-start) | copy-done | bytes 98328
  1.5 0.0 copy-start.1
  1.5 0.9 %copy-done.1 = f32[3,4,2,8,128]{4,3,2,1,0:T(8,128)S(1)} copy-done((f32[3,4,2,8,128]{4,3,2,1,0:T(8,128)S(1)}, f32[3,4,2,8,128]{4,3,2,1,0:T(8,128)}, u32[]{:S(2)}) %copy-start.1) | copy-done | bytes 98328
  2.4 0.0 copy-start.2
  2.4 0.8 %copy-done.2 = s32[2,4,2,8,128]{4,3,2,1,0:T(8,128)S(1)} copy-done((s32[2,4,2,8,128]{4,3,2,1,0:T(8,128)S(1)}, s32[2,4,2,8,128]{4,3,2,1,0:T(8,128)}, u32[]{:S(2)}) %copy-start.2) | copy-done | bytes 65560
  3.3 0.0 copy-start.3
  3.3 0.8 copy-done.3
  4.0 0.0 copy-start.4
  4.0 0.8 copy-done.4
  4.8 72.1 %shard_map.76 = (f32[3,4,2,8,128]{4,3,2,1,0:T(8,128)S(1)}, f32[3,4,2,8,128]{4,3,2,1,0:T(8,128)S(1)}, f32[3,4,2,8,128]{4,3,2,1,0:T(8,128)S(1)}) custom-call(f32[3,4,2,8,128]{4,3,2,1,0:T(8,128)S(1)} %copy-done, f32[3,4,2,8,128]{4,3,2,1,0:T(8,128)S(1)} %copy-done.1, s32[4,2,8,128]{3,2,1,0:T(8,128)S(1)} %copy-done.3, s32[2,4,2,8,128]{4,3,2,1,0:T(8,128)S(1)} %copy-done.2, ...), custom_call_target="tpu_custom_call" | custom-call | tf_op jit(solution)/shard_map/pallas_call | solution.py:424
  76.9 0.6 copy.11
  77.6 0.6 copy.12
  78.2 0.6 copy.13
Async XLA Ops:
  0.6 0.9 %copy-start = (f32[3,4,2,8,128]{4,3,2,1,0:T(8,128)S(1)}, f32[3,4,2,8,128]{4,3,2,1,0:T(8,128)}, u32[]{:S(2)}) copy-start(f32[3,4,2,8,128]{4,3,2,1,0:T(8,128)} %off_in.1) | copy-start | bytes 294916
  1.5 0.9 %copy-start.1 = (f32[3,4,2,8,128]{4,3,2,1,0:T(8,128)S(1)}, f32[3,4,2,8,128]{4,3,2,1,0:T(8,128)}, u32[]{:S(2)}) copy-start(f32[3,4,2,8,128]{4,3,2,1,0:T(8,128)} %vel_in.1) | copy-start | bytes 294916
  2.4 0.8 %copy-start.2 = (s32[2,4,2,8,128]{4,3,2,1,0:T(8,128)S(1)}, s32[2,4,2,8,128]{4,3,2,1,0:T(8,128)}, u32[]{:S(2)}) copy-start(s32[2,4,2,8,128]{4,3,2,1,0:T(8,128)} %par_in.1) | copy-start | bytes 196612
  3.3 0.8 copy-start.3
  4.0 0.8 copy-start.4

commit v2 on v1

--- a/solution.py
+++ b/solution.py
@@ -78,7 +78,7 @@
         plane_peers.append((there % NSLAB, (there // NSLAB) * HALF + low))
 
     barrier = pltpu.get_barrier_semaphore()
-    everyone = near + line + plane_peers
+    everyone = plane_peers[::-1] + line + near
     for device in everyone:
         pl.semaphore_signal(barrier, inc=1, device_id=device, device_id_type=MESH)
 
@@ -114,13 +114,13 @@
             for c in (1, 2):
                 box[0, p + 1, c * SLOTS + j, 8:16, :] = off[c, j, p]
 
-    def pack(e):
+    def pack(e, p):
         for side, row in ((0, 8), (1, 15)):
-            for p in range(2):
-                for k in range(PARTS):
-                    rows_out[e, side, p, k : k + 1, :] = box[e, p + 1, k, row : row + 1, :]
-
-    pack(0)
+            for k in range(PARTS):
+                rows_out[e, side, p, k : k + 1, :] = box[e, p + 1, k, row : row + 1, :]
+
+    pack(0, 0)
+    pack(0, 1)
     for side, row in ((0, 8), (1, 15)):
         for p in range(2):
             for j in range(SLOTS):
@@ -151,49 +151,52 @@
 
     pl.semaphore_wait(barrier, len(everyone))
 
-    def face(e, k, source, target):
+    def send(e, k, to, source, target):
         return pltpu.make_async_remote_copy(
             src_ref=source,
             dst_ref=target,
             send_sem=face_send.at[e, k],
             recv_sem=face_recv.at[e, k],
-            device_id=near[k % 8],
+            device_id=near[around.index(to)],
             device_id_type=MESH,
         )
 
-    def planes(e, p):
-        return face(
-            e,
-            1 - p,
-            box.at[e, p + 1, :, 8:16, :],
-            box.at[e, 3 - 3 * p, :, 8:16, :],
+    def face(e, p):
+        x = 2 * p - 1
+        own, far = box.at[e, p + 1, :, 8:16, :], box.at[e, 3 - 3 * p, :, 8:16, :]
+        return send(e, 5 * p, (x, 0), own, far)
+
+    def edges(e, p):
+        x, q = 2 * p - 1, 3 - 3 * p
+        out = []
+        for side, y in ((0, -1), (1, 1)):
+            rows, here = rows_out.at[e, side, p], rows_in.at[e, 1 - side]
+            out.append(send(e, 5 * p + 1 + side, (0, y), rows, here.at[p + 1]))
+            out.append(send(e, 5 * p + 3 + side, (x, y), rows, here.at[q]))
+        return out
+
+    label_faces = [
+        send(
+            0,
+            10 + p,
+            (2 * p - 1, 0),
+            labels.at[p + 1, :, 8:16, :],
+            labels.at[3 - 3 * p, :, 8:16, :],
         )
-
-    def edges(e):
-        return [
-            face(e, 2, rows_out.at[e, 1], rows_in.at[e, 0, 1:3]),
-            face(e, 3, rows_out.at[e, 0], rows_in.at[e, 1, 1:3]),
-            face(e, 4, rows_out.at[e, 1, 1], rows_in.at[e, 0, 0]),
-            face(e, 5, rows_out.at[e, 0, 1], rows_in.at[e, 1, 0]),
-            face(e, 6, rows_out.at[e, 1, 0], rows_in.at[e, 0, 3]),
-            face(e, 7, rows_out.at[e, 0, 0], rows_in.at[e, 1, 3]),
-        ]
-
-    label_faces = [
-        face(0, 9 - p, labels.at[p + 1, :, 8:16, :], labels.at[3 - 3 * p, :, 8:16, :])
         for p in range(2)
     ]
-    face_copies = [[planes(e, 0), planes(e, 1)] for e in range(4)]
-    edge_copies = [edges(e) for e in range(4)]
-
-    def unpack(e):
-        def one(q, carry):
+    face_copies = [[face(e, p) for p in range(2)] for e in range(4)]
+    edge_copies = [[edges(e, p) for p in range(2)] for e in range(4)]
+
+    def unpack(e, p):
+        def one(t, carry):
+            q = (1 + 2 * t) if p == 0 else (2 - 2 * t)
             for side, row in ((0, 7), (1, 16)):
                 for k in range(PARTS):
                     box[e, q, k, row : row + 1, :] = rows_in[e, side, q, k : k + 1, :]
             return carry
 
-        lax.fori_loop(0, 4, one, 0)
+        lax.fori_loop(0, 2, one, 0)
 
     def group(e, p, q, ey, fresh):
         ex = (q - p - 1).astype(jnp.float32) * cell_width
@@ -250,21 +253,18 @@
         lax.fori_loop(0, 2, first, 0)
         lax.fori_loop(0, 2, second, 0)
 
-    def sides(e):
+    def sides(e, pairs):
         def one(t, carry):
+            p, q = pairs(t)
             for ey in (-1, 1):
-                group(e, t // 2, 1 + t % 2, ey, False)
+                group(e, p, q, ey, False)
             return carry
 
-        lax.fori_loop(0, 4, one, 0)
-
-    def outer(e):
-        def one(p, carry):
-            for ey in (-1, 0, 1):
-                group(e, p, 3 * p, ey, False)
-            return carry
-
-        lax.fori_loop(0, 2, one, 0)
+        return one
+
+    def outer(e, p):
+        for ey in (-1, 0, 1):
+            group(e, p, 3 * p, ey, False)
 
     def limits():
         def one(t, carry):
@@ -309,17 +309,17 @@
             base += len(peers)
         yield jnp.max(row, axis=1, keepdims=True)
 
-    for copy in face_copies[0] + edge_copies[0] + label_faces:
+    for copy in face_copies[0] + edge_copies[0][0] + edge_copies[0][1] + label_faces:
         copy.start()
     inner(0)
-    for copy in edge_copies[0]:
-        copy.wait_recv()
-    unpack(0)
-    sides(0)
-    for copy in face_copies[0]:
-        copy.wait_recv()
-    outer(0)
     for p in range(2):
+        for copy in edge_copies[0][p]:
+            copy.wait_recv()
+        unpack(0, p)
+    for p in range(2):
+        lax.fori_loop(0, 2, sides(0, lambda t: (jnp.int32(p), 1 + t)), 0)
+        face_copies[0][1 - p].wait_recv()
+        outer(0, jnp.int32(p))
         for c in range(3):
             for i in range(SLOTS):
                 k = c * SLOTS + i
@@ -330,9 +330,9 @@
                     time_step * moving + half_step_sq * force
                 )
         face_copies[1][p].start()
-    pack(1)
-    for copy in edge_copies[1]:
-        copy.start()
+        pack(1, p)
+        for copy in edge_copies[1][p]:
+            copy.start()
     for copy in label_faces:
         copy.wait_recv()
 
@@ -347,19 +347,27 @@
     lax.fori_loop(0, 4, label_rows, 0)
     limits()
     inner(1)
-    for copy in edge_copies[1]:
-        copy.wait_recv()
-    unpack(1)
-    sides(1)
-    for copy in face_copies[1]:
-        copy.wait_recv()
-
-    started = face_copies[0] + edge_copies[0] + label_faces + edge_copies[1]
+    for p in range(2):
+        for copy in edge_copies[1][p]:
+            copy.wait_recv()
+        unpack(1, p)
+        lax.fori_loop(0, 2, sides(1, lambda t: (t, jnp.int32(p + 1))), 0)
+        face_copies[1][p].wait_recv()
+        outer(1, jnp.int32(1 - p))
+
+    started = face_copies[0] + label_faces
+    for e in range(2):
+        started += edge_copies[e][0] + edge_copies[e][1]
     for r in range(3):
         if r > 0:
             inner(1)
-            sides(1)
-        outer(1)
+            lax.fori_loop(0, 4, sides(1, lambda t: (t // 2, 1 + t % 2)), 0)
+
+            def far(p, carry):
+                outer(1, p)
+                return carry
+
+            lax.fori_loop(0, 2, far, 0)
         final = r == 2
         peak = jnp.zeros((8, 128), jnp.float32)
         for p in range(2):
@@ -377,19 +385,19 @@
         steps = global_max(r, peak)
         started += next(steps)
         if not final:
-            for copy in face_copies[r + 2]:
-                copy.start()
-            pack(r + 2)
-            for copy in edge_copies[r + 2]:
-                copy.start()
-            started += face_copies[r + 2] + edge_copies[r + 2]
+            for p in range(2):
+                face_copies[r + 2][p].start()
+                pack(r + 2, p)
+                for copy in edge_copies[r + 2][p]:
+                    copy.start()
+                started += [face_copies[r + 2][p]] + edge_copies[r + 2][p]
         started += next(steps)
         if not final:
-            for copy in edge_copies[r + 2]:
-                copy.wait_recv()
-            unpack(r + 2)
-            for copy in face_copies[r + 2]:
-                copy.wait_recv()
+            for p in range(2):
+                for copy in edge_copies[r + 2][p]:
+                    copy.wait_recv()
+                unpack(r + 2, p)
+                face_copies[r + 2][p].wait_recv()
         largest = next(steps)
         inverse = 1.0 / (jnp.sqrt(largest) + tiny_eps)
         scale = step_length * inverse
@@ -417,41 +425,62 @@
         copy.wait_send()
 
 
+def store(pos, half, unit, pos_out, half_out, unit_out, sem):
+    copies = [
+        pltpu.make_async_copy(source, target, sem.at[k])
+        for k, (source, target) in enumerate(
+            ((pos, pos_out), (half, half_out), (unit, unit_out))
+        )
+    ]
+    for copy in copies:
+        copy.start()
+    for copy in copies:
+        copy.wait()
+
+
 def shards(offsets, velocities, chain_label, partners, anchored):
-    shape = jax.ShapeDtypeStruct(offsets.shape, jnp.float32)
     f32 = jnp.float32
+    shape = offsets.shape
+    parts = pl.pallas_call(
+        kernel,
+        out_shape=(pltpu.VMEM(shape, f32),) * 3,
+        in_specs=[pl.BlockSpec(memory_space=pl.ANY)] * 5,
+        out_specs=[pl.BlockSpec(memory_space=pltpu.VMEM)] * 3,
+        scratch_shapes=[
+            pltpu.VMEM(shape, f32),
+            pltpu.VMEM(shape, f32),
+            pltpu.VMEM(chain_label.shape, jnp.int32),
+            pltpu.VMEM(partners.shape, jnp.int32),
+            pltpu.VMEM(anchored.shape, jnp.int32),
+            pltpu.VMEM((4, 4, PARTS, 24, 128), f32),
+            pltpu.VMEM((4, SLOTS, 24, 128), f32),
+            pltpu.VMEM((4, 2, 2, 16, 128), f32),
+            pltpu.VMEM((4, 2, 4, 16, 128), f32),
+            pltpu.VMEM((2, 9, 3, SLOTS, SLOTS, 8, 128), f32),
+            pltpu.VMEM((2, 9, 3, SLOTS, SLOTS, 8, 128), f32),
+            pltpu.VMEM((2, PARTS, 8, 128), f32),
+            pltpu.VMEM((2, SLOTS, 8, 128), f32),
+            pltpu.VMEM((3, 2, 1, 128), f32),
+            pltpu.VMEM((3, N1 + N2, 1, 128), f32),
+            pltpu.SemaphoreType.DMA((5,)),
+            pltpu.SemaphoreType.DMA((4, 12)),
+            pltpu.SemaphoreType.DMA((4, 12)),
+            pltpu.SemaphoreType.DMA((3, N1 + N2)),
+            pltpu.SemaphoreType.DMA((3, N1 + N2)),
+        ],
+        compiler_params=pltpu.CompilerParams(
+            collective_id=0, has_side_effects=True, vmem_limit_bytes=60 * 1024 * 1024
+        ),
+    )(offsets, velocities, chain_label, partners, anchored)
     return tuple(
         pl.pallas_call(
-            kernel,
-            out_shape=(shape, shape, shape),
-            in_specs=[pl.BlockSpec(memory_space=pl.ANY)] * 5,
-            out_specs=[pl.BlockSpec(memory_space=pltpu.VMEM)] * 3,
-            scratch_shapes=[
-                pltpu.VMEM(offsets.shape, f32),
-                pltpu.VMEM(velocities.shape, f32),
-                pltpu.VMEM(chain_label.shape, jnp.int32),
-                pltpu.VMEM(partners.shape, jnp.int32),
-                pltpu.VMEM(anchored.shape, jnp.int32),
-                pltpu.VMEM((4, 4, PARTS, 24, 128), f32),
-                pltpu.VMEM((4, SLOTS, 24, 128), f32),
-                pltpu.VMEM((4, 2, 2, 16, 128), f32),
-                pltpu.VMEM((4, 2, 4, 16, 128), f32),
-                pltpu.VMEM((2, 9, 3, SLOTS, SLOTS, 8, 128), f32),
-                pltpu.VMEM((2, 9, 3, SLOTS, SLOTS, 8, 128), f32),
-                pltpu.VMEM((2, PARTS, 8, 128), f32),
-                pltpu.VMEM((2, SLOTS, 8, 128), f32),
-                pltpu.VMEM((3, 2, 1, 128), f32),
-                pltpu.VMEM((3, N1 + N2, 1, 128), f32),
-                pltpu.SemaphoreType.DMA((5,)),
-                pltpu.SemaphoreType.DMA((4, 10)),
-                pltpu.SemaphoreType.DMA((4, 10)),
-                pltpu.SemaphoreType.DMA((3, N1 + N2)),
-                pltpu.SemaphoreType.DMA((3, N1 + N2)),
-            ],
-            compiler_params=pltpu.CompilerParams(
-                collective_id=0, has_side_effects=True, vmem_limit_bytes=24 * 1024 * 1024
-            ),
-        )(offsets, velocities, chain_label, partners, anchored)
+            store,
+            out_shape=(jax.ShapeDtypeStruct(shape, f32),) * 3,
+            in_specs=[pl.BlockSpec(memory_space=pl.ANY)] * 3,
+            out_specs=[pl.BlockSpec(memory_space=pl.ANY)] * 3,
+            scratch_shapes=[pltpu.SemaphoreType.DMA((3,))],
+            compiler_params=pltpu.CompilerParams(vmem_limit_bytes=1024 * 1024),
+        )(*parts)
     )
 
 

time: 79.2 us -> 72.7 us (0.918)
  local copies, waits for them, and re-layouts: 6.05 us -> 0 us
    unnamed x13 -> x0, local copies, waits for them, and re-layouts: 6.05 us -> none
    pallas_call x1 -> x2, Pallas kernels: 72.1 us -> 71.9 us  [the longest x1 71.2 us: shards(): pl.pallas_call(kernel, out_shape=(pltpu.VMEM(shape, f32),) * 3, in_specs=...]
where the time goes in v2:
time: 72.7 us; the launch traced here: 72.5 us
  Pallas kernels  71.9 us (99%)
    pallas_call x1, Pallas kernels, shards(): pl.pallas_call(kernel, out_shape=(pltpu.VMEM(shape, f32),) * 3, in_specs=...  71.2 us

profile of v2, /device:TPU:1, one launch (start us, length us, event | category | flops | bytes accessed | tf_op | source)
XLA Modules:
  0.0 72.5 jit_solution(17195980590635317730)
XLA Ops:
  0.6 71.2 %shard_map.76 = (f32[3,4,2,8,128]{4,3,2,1,0:T(8,128)S(1)}, f32[3,4,2,8,128]{4,3,2,1,0:T(8,128)S(1)}, f32[3,4,2,8,128]{4,3,2,1,0:T(8,128)S(1)}) custom-call(f32[3,4,2,8,128]{4,3,2,1,0:T(8,128)} %off_in.1, f32[3,4,2,8,128]{4,3,2,1,0:T(8,128)} %vel_in.1, s32[4,2,8,128]{3,2,1,0:T(8,128)} %lab_in.1, s32[2,4,2,8,128]{4,3,2,1,0:T(8,128)} %par_in.1, ...), custom_call_target="tpu_custom_call" | custom-call | tf_op jit(solution)/shard_map/pallas_call | solution.py:444
  71.8 0.7 %shard_map.77 = (f32[3,4,2,8,128]{4,3,2,1,0:T(8,128)}, f32[3,4,2,8,128]{4,3,2,1,0:T(8,128)}, f32[3,4,2,8,128]{4,3,2,1,0:T(8,128)}) custom-call(f32[3,4,2,8,128]{4,3,2,1,0:T(8,128)S(1)} %get-tuple-element.6.pos, f32[3,4,2,8,128]{4,3,2,1,0:T(8,128)S(1)} %get-tuple-element.7.half, f32[3,4,2,8,128]{4,3,2,1,0:T(8,128)S(1)} %get-tuple-element.8.unit), custom_call_target="tpu_custom_call" | custom-call | tf_op jit(solution)/shard_map/pallas_call | solution.py:476

commit v3 on v2

--- a/solution.py
+++ b/solution.py
@@ -9,8 +9,27 @@
 SLOTS = 4
 PARTS = 12
 NSLAB, NSUB = 16, 32
-HALF = 16
-N1, N2 = 15, 31
+
+
+def hops(offset):
+    dx, dy, dz, _ = offset
+    return min(dx, 4 - dx) + min(dy, 8 - dy) + min(dz, 8 - dz)
+
+
+LINE = [(0, 0, dz, dc) for dz in range(8) for dc in range(2) if dz + dc > 0]
+PLANE = [(dx, dy, 0, 0) for dx in range(4) for dy in range(8) if dx + dy > 0]
+FAR = [
+    (dx, dy, dz, dc)
+    for dx, dy, _, _ in PLANE
+    for dz in (3, 4, 5)
+    for dc in range(2)
+    if hops((dx, dy, dz, dc)) >= 9
+]
+PEERS = LINE + PLANE + FAR
+ROUTE = sorted(range(len(PEERS)), key=lambda k: -hops(PEERS[k]))
+LINE_KEYS = [k for k in ROUTE if k < len(LINE)]
+PLANE_KEYS = [k for k in ROUTE if len(LINE) <= k < len(LINE) + len(PLANE)]
+FAR_KEYS = [k for k in ROUTE if k >= len(LINE) + len(PLANE)]
 
 cell_width = 1.25
 soft_floor = 0.64
@@ -69,16 +88,16 @@
         (-1, -1),
     )
     near = [((slab + u + NSLAB) % NSLAB, (sub + v + NSUB) % NSUB) for u, v in around]
-    low, part = sub % HALF, sub // HALF
-    line = [(slab, part * HALF + (low + d) % HALF) for d in range(1, N1 + 1)]
-    place = part * NSLAB + slab
-    plane_peers = []
-    for d in range(1, N2 + 1):
-        there = (place + d) % (NSLAB * 2)
-        plane_peers.append((there % NSLAB, (there // NSLAB) * HALF + low))
+    x, y = (slab // 8) * 2 + sub // 16, slab % 8
+    z, core = (sub // 2) % 8, sub % 2
+    peers = []
+    for dx, dy, dz, dc in PEERS:
+        there = (x + dx) % 4
+        z_core = ((z + dz) % 8) * 2 + (core + dc) % 2
+        peers.append(((there // 2) * 8 + (y + dy) % 8, (there % 2) * 16 + z_core))
 
     barrier = pltpu.get_barrier_semaphore()
-    everyone = plane_peers[::-1] + line + near
+    everyone = [peers[k] for k in ROUTE] + near
     for device in everyone:
         pl.semaphore_signal(barrier, inc=1, device_id=device, device_id_type=MESH)
 
@@ -286,27 +305,41 @@
 
     def global_max(r, value):
         row = jnp.max(value, axis=0, keepdims=True)
-        base = 0
-        for phase, peers in enumerate((line, plane_peers)):
-            mine[r, phase] = row
-            copies = [
-                pltpu.make_async_remote_copy(
-                    src_ref=mine.at[r, phase],
-                    dst_ref=slots.at[r, base + k],
-                    send_sem=max_send.at[r, base + k],
-                    recv_sem=max_recv.at[r, base + k],
-                    device_id=device,
+        waiting = {}
+
+        def tell(stage, keys):
+            mine[r, stage] = row
+            for k in keys:
+                waiting[k] = pltpu.make_async_remote_copy(
+                    src_ref=mine.at[r, stage],
+                    dst_ref=slots.at[r, k],
+                    send_sem=max_send.at[r, k],
+                    recv_sem=max_recv.at[r, k],
+                    device_id=peers[k],
                     device_id_type=MESH,
                 )
-                for k, device in enumerate(peers)
-            ]
-            for copy in copies:
-                copy.start()
-            yield copies
-            for copy in copies:
-                copy.wait_recv()
-            row = jnp.maximum(row, jnp.max(slots[r, base : base + len(peers)], axis=0))
-            base += len(peers)
+                waiting[k].start()
+
+        tell(0, LINE_KEYS + FAR_KEYS)
+        yield []
+        for stage, (nearest, farthest) in enumerate(((0, 2), (3, 3), (4, 4))):
+            heard = [k for k in LINE_KEYS if nearest <= hops(PEERS[k]) <= farthest]
+            for k in heard:
+                waiting[k].wait_recv()
+            for k in heard:
+                row = jnp.maximum(row, slots[r, k])
+            tell(
+                stage + 1,
+                [
+                    k
+                    for k in PLANE_KEYS
+                    if hops(PEERS[k]) == 6 - stage or (stage == 2 and hops(PEERS[k]) < 4)
+                ],
+            )
+        yield list(waiting.values())
+        for k in PLANE_KEYS[::-1] + FAR_KEYS:
+            waiting[k].wait_recv()
+        row = jnp.maximum(row, jnp.max(slots[r, len(LINE) :], axis=0))
         yield jnp.max(row, axis=1, keepdims=True)
 
     for copy in face_copies[0] + edge_copies[0][0] + edge_copies[0][1] + label_faces:
@@ -460,13 +493,13 @@
             pltpu.VMEM((2, 9, 3, SLOTS, SLOTS, 8, 128), f32),
             pltpu.VMEM((2, PARTS, 8, 128), f32),
             pltpu.VMEM((2, SLOTS, 8, 128), f32),
-            pltpu.VMEM((3, 2, 1, 128), f32),
-            pltpu.VMEM((3, N1 + N2, 1, 128), f32),
+            pltpu.VMEM((3, 4, 1, 128), f32),
+            pltpu.VMEM((3, len(PEERS), 1, 128), f32),
             pltpu.SemaphoreType.DMA((5,)),
             pltpu.SemaphoreType.DMA((4, 12)),
             pltpu.SemaphoreType.DMA((4, 12)),
-            pltpu.SemaphoreType.DMA((3, N1 + N2)),
-            pltpu.SemaphoreType.DMA((3, N1 + N2)),
+            pltpu.SemaphoreType.DMA((3, len(PEERS))),
+            pltpu.SemaphoreType.DMA((3, len(PEERS))),
         ],
         compiler_params=pltpu.CompilerParams(
             collective_id=0, has_side_effects=True, vmem_limit_bytes=60 * 1024 * 1024

time: 72.7 us -> 75.4 us (1.037)
  Pallas kernels: 71.9 us -> 74.6 us
    pallas_call x1, Pallas kernels: 71.2 us -> 73.9 us  [shards(): pl.pallas_call(kernel, out_shape=(pltpu.VMEM(shape, f32),) * 3, in_specs=...]
where the time goes in v3:
time: 75.4 us; the launch traced here: 75.2 us
  Pallas kernels  74.6 us (99%)
    pallas_call x1, Pallas kernels, shards(): pl.pallas_call(kernel, out_shape=(pltpu.VMEM(shape, f32),) * 3, in_specs=...  73.9 us

profile of v3, /device:TPU:1, one launch (start us, length us, event | category | flops | bytes accessed | tf_op | source)
XLA Modules:
  0.0 75.2 jit_solution(16078996899595958622)
XLA Ops:
  0.6 73.9 %shard_map.76 = (f32[3,4,2,8,128]{4,3,2,1,0:T(8,128)S(1)}, f32[3,4,2,8,128]{4,3,2,1,0:T(8,128)S(1)}, f32[3,4,2,8,128]{4,3,2,1,0:T(8,128)S(1)}) custom-call(f32[3,4,2,8,128]{4,3,2,1,0:T(8,128)} %off_in.1, f32[3,4,2,8,128]{4,3,2,1,0:T(8,128)} %vel_in.1, s32[4,2,8,128]{3,2,1,0:T(8,128)} %lab_in.1, s32[2,4,2,8,128]{4,3,2,1,0:T(8,128)} %par_in.1, ...), custom_call_target="tpu_custom_call" | custom-call | tf_op jit(solution)/shard_map/pallas_call | solution.py:477
  74.5 0.7 shard_map.77

commit v4 on v2

--- a/solution.py
+++ b/solution.py
@@ -11,6 +11,9 @@
 NSLAB, NSUB = 16, 32
 HALF = 16
 N1, N2 = 15, 31
+
+LINE_STEPS = sorted(range(1, N1 + 1), key=lambda d: -min(d, HALF - d))
+PLANE_STEPS = sorted(range(1, N2 + 1), key=lambda d: -min(d % 8, 8 - d % 8))
 
 cell_width = 1.25
 soft_floor = 0.64
@@ -70,15 +73,15 @@
     )
     near = [((slab + u + NSLAB) % NSLAB, (sub + v + NSUB) % NSUB) for u, v in around]
     low, part = sub % HALF, sub // HALF
-    line = [(slab, part * HALF + (low + d) % HALF) for d in range(1, N1 + 1)]
+    line = [(slab, part * HALF + (low + d) % HALF) for d in LINE_STEPS]
     place = part * NSLAB + slab
     plane_peers = []
-    for d in range(1, N2 + 1):
+    for d in PLANE_STEPS:
         there = (place + d) % (NSLAB * 2)
         plane_peers.append((there % NSLAB, (there // NSLAB) * HALF + low))
 
     barrier = pltpu.get_barrier_semaphore()
-    everyone = plane_peers[::-1] + line + near
+    everyone = plane_peers + line + near
     for device in everyone:
         pl.semaphore_signal(barrier, inc=1, device_id=device, device_id_type=MESH)
 

time: 72.7 us -> 72.4 us (level)
  no operation moved by 1% of the time
where the time goes in v4:
time: 72.4 us; the launch traced here: 72.3 us
  Pallas kernels  71.6 us (99%)
    pallas_call x1, Pallas kernels, shards(): pl.pallas_call(kernel, out_shape=(pltpu.VMEM(shape, f32),) * 3, in_specs=...  70.9 us

profile of v4, /device:TPU:1, one launch (start us, length us, event | category | flops | bytes accessed | tf_op | source)
XLA Modules:
  0.0 72.3 jit_solution(7246131846113013754)
XLA Ops:
  0.6 70.9 %shard_map.76 = (f32[3,4,2,8,128]{4,3,2,1,0:T(8,128)S(1)}, f32[3,4,2,8,128]{4,3,2,1,0:T(8,128)S(1)}, f32[3,4,2,8,128]{4,3,2,1,0:T(8,128)S(1)}) custom-call(f32[3,4,2,8,128]{4,3,2,1,0:T(8,128)} %off_in.1, f32[3,4,2,8,128]{4,3,2,1,0:T(8,128)} %vel_in.1, s32[4,2,8,128]{3,2,1,0:T(8,128)} %lab_in.1, s32[2,4,2,8,128]{4,3,2,1,0:T(8,128)} %par_in.1, ...), custom_call_target="tpu_custom_call" | custom-call | tf_op jit(solution)/shard_map/pallas_call | solution.py:447
  71.5 0.7 %shard_map.77 = (f32[3,4,2,8,128]{4,3,2,1,0:T(8,128)}, f32[3,4,2,8,128]{4,3,2,1,0:T(8,128)}, f32[3,4,2,8,128]{4,3,2,1,0:T(8,128)}) custom-call(f32[3,4,2,8,128]{4,3,2,1,0:T(8,128)S(1)} %get-tuple-element.6.pos, f32[3,4,2,8,128]{4,3,2,1,0:T(8,128)S(1)} %get-tuple-element.7.half, f32[3,4,2,8,128]{4,3,2,1,0:T(8,128)S(1)} %get-tuple-element.8.unit), custom_call_target="tpu_custom_call" | custom-call | tf_op jit(solution)/shard_map/pallas_call | solution.py:479
